TPU v7x, 256 devices: a whole 4x4x8 slice. The times are simulated.
256 devices in a mesh: pair: 2 (over y_hi), tm: 8 (over z), fsdp: 16 (over y_lo, x, core).
Axes of the slice: x: 4, y: 4 (y_hi: 2, y_lo: 2; y = y_hi * 2 + y_lo), z: 8, core: 2. Of those that a mesh axis runs over, the one named last changes fastest.
Arguments:
- frames: bfloat16 [2, 64, 1024, 1536], P('pair', 'tm', 'fsdp'), may hold values from -8 to 8
- frame_time: int32 [2, 64], P('pair'), may hold values from 0 to 63, as said below
- w_qkv: bfloat16 [1536, 2304], P('fsdp'), may hold values from -1 to 1
- w_out: bfloat16 [768, 1536], P(None, 'fsdp'), may hold values from -0.21875 to 0.21875
- grad_out: bfloat16 [2, 64, 1024, 1536], P('pair', 'tm', 'fsdp'), may hold values from -6 to 6
Outputs:
- grad_frames: bfloat16 [2, 64, 1024, 1536], P('pair', 'tm', 'fsdp')
- grad_qkv: float32 [1536, 2304], P('fsdp')
- grad_out_weight: float32 [768, 1536], P(None, 'fsdp')
Inputs may be any that keep to these rules, and one draw needn't show every extreme that they name: `frame_time`: Non-decreasing along the frames of a clip, 0 at its first frame and 63 at its last; equal values mark frames of one time step.
All inputs are finite; a program needn't handle non-finite values.
Results may differ from a plain program's by a relative error of at most 0.04.
The roundings to bfloat16 on the way count: a program that leaves them out, or rounds other values in their place, can miss the bound.
Values may be sent and summed in bfloat16 or wider, within the bound.
No kernel may reach another device: no remote copies, remote signals or barrier semaphores. Data moves between devices by JAX's collectives and lax.ppermute only.
A program may use at most 128 MiB of HBM per device.

v0:
```python
import math

import jax
import jax.numpy as jnp
from jax import lax
from jax.sharding import PartitionSpec as P

HEAD_DIM = 64


def norm_parts(frames_in):
    float_rows = frames_in.astype(jnp.float32)
    inv_rms = lax.rsqrt(jnp.mean(float_rows * float_rows, axis=-1, keepdims=True) + 1e-06)
    normed = (float_rows * inv_rms).astype(jnp.bfloat16)
    return (float_rows, inv_rms, normed)


def attention_forward(qkv, frame_times):
    clips_here, frames_here, patches_here, triple = qkv.shape
    head_count = triple // (3 * HEAD_DIM)
    split_qkv = qkv.reshape(clips_here, frames_here, patches_here, 3, head_count, HEAD_DIM)
    queries = split_qkv[:, :, :, 0]
    key_rows = split_qkv[:, :, :, 1]
    values = split_qkv[:, :, :, 2]
    scores = jnp.einsum(
        "ciphd,cjphd->cphij", queries, key_rows, preferred_element_type=jnp.float32
    ) * HEAD_DIM ** (-0.5)
    allowed = frame_times[:, None, :] <= frame_times[:, :, None]
    scores = jnp.where(allowed[:, None, None, :, :], scores, -1e30)
    row_max = jnp.max(scores, axis=-1, keepdims=True)
    exponent = jnp.exp(scores - row_max)
    weights = exponent / jnp.sum(exponent, axis=-1, keepdims=True)
    rounded_weights = weights.astype(jnp.bfloat16)
    mixed_rows = jnp.einsum(
        "cphij,cjphd->ciphd", rounded_weights, values, preferred_element_type=jnp.float32
    )
    mixed_rows = mixed_rows.astype(jnp.bfloat16).reshape(
        clips_here, frames_here, patches_here, head_count * HEAD_DIM
    )
    return (mixed_rows, weights, rounded_weights, split_qkv)


def attention_backward(d_mixed, weights, rounded_weights, split_qkv):
    clips_here, frames_here, patches_here, inner_width = d_mixed.shape
    head_count = inner_width // HEAD_DIM
    d_heads = d_mixed.reshape(clips_here, frames_here, patches_here, head_count, HEAD_DIM)
    queries = split_qkv[:, :, :, 0]
    key_rows = split_qkv[:, :, :, 1]
    values = split_qkv[:, :, :, 2]
    d_weights = jnp.einsum(
        "ciphd,cjphd->cphij", d_heads, values, preferred_element_type=jnp.float32
    )
    centered = d_weights - jnp.sum(weights * d_weights, axis=-1, keepdims=True)
    d_scores = (weights * centered * HEAD_DIM ** (-0.5)).astype(jnp.bfloat16)
    d_query = jnp.einsum(
        "cphij,cjphd->ciphd", d_scores, key_rows, preferred_element_type=jnp.float32
    ).astype(jnp.bfloat16)
    d_key = jnp.einsum(
        "cphij,ciphd->cjphd", d_scores, queries, preferred_element_type=jnp.float32
    ).astype(jnp.bfloat16)
    d_value = jnp.einsum(
        "cphij,ciphd->cjphd", rounded_weights, d_heads, preferred_element_type=jnp.float32
    ).astype(jnp.bfloat16)
    stacked = jnp.stack([d_query, d_key, d_value], axis=3)
    return stacked.reshape(clips_here, frames_here, patches_here, 3 * inner_width)


def outer_sum(left_rows, right_rows):
    return lax.dot_general(
        left_rows, right_rows, (((0,), (0,)), ((), ())), preferred_element_type=jnp.float32
    )


def finish_local(flat_normed, d_qkv, mixed_rows, grad_block, float_rows, inv_rms, full_qkv):
    inner_width = mixed_rows.shape[-1]
    qkv_rows = d_qkv.reshape(-1, 3 * inner_width)
    grad_rows = grad_block.reshape(-1, grad_block.shape[-1])
    term_qkv = outer_sum(flat_normed, qkv_rows)
    term_out = outer_sum(mixed_rows.reshape(-1, inner_width), grad_rows)
    d_normed = lax.dot_general(
        qkv_rows, full_qkv, (((1,), (1,)), ((), ())), preferred_element_type=jnp.float32
    )
    d_normed = d_normed.reshape(float_rows.shape)
    scaled = float_rows * inv_rms
    inner_term = jnp.mean(d_normed * scaled, axis=-1, keepdims=True)
    grad_local = (
        grad_block.astype(jnp.float32) + inv_rms * (d_normed - scaled * inner_term)
    ).astype(jnp.bfloat16)
    return (term_qkv, term_out, grad_local)


def on_device(frames, frame_time, w_qkv, w_out, grad_out):
    inner_width = w_out.shape[0]
    full_qkv, full_out = (
        lax.all_gather(w_qkv, "fsdp", axis=0, tiled=True),
        lax.all_gather(w_out, "fsdp", axis=1, tiled=True),
    )
    float_rows, inv_rms, normed = norm_parts(frames)
    flat_normed = normed.reshape(-1, normed.shape[-1])
    qkv = jnp.dot(flat_normed, full_qkv, preferred_element_type=jnp.float32).astype(jnp.bfloat16)
    qkv = qkv.reshape(frames.shape[:3] + (3 * inner_width,))
    qkv_here = lax.all_to_all(qkv, "tm", split_axis=2, concat_axis=1, tiled=True)
    mixed_here, weights, rounded_weights, split_qkv = attention_forward(qkv_here, frame_time)
    mixed_rows = lax.all_to_all(mixed_here, "tm", split_axis=1, concat_axis=2, tiled=True)
    grad_rows = grad_out.reshape(-1, grad_out.shape[-1])
    d_mixed = (
        jnp.dot(grad_rows, full_out.T, preferred_element_type=jnp.float32)
        .astype(jnp.bfloat16)
        .reshape(frames.shape[:3] + (inner_width,))
    )
    d_mixed_here = lax.all_to_all(d_mixed, "tm", split_axis=2, concat_axis=1, tiled=True)
    d_qkv_here = attention_backward(d_mixed_here, weights, rounded_weights, split_qkv)
    d_qkv = lax.all_to_all(d_qkv_here, "tm", split_axis=1, concat_axis=2, tiled=True)
    term_qkv, term_out, grad_frames = finish_local(
        flat_normed, d_qkv, mixed_rows, grad_out, float_rows, inv_rms, full_qkv
    )
    shard_qkv, shard_out = (
        lax.psum_scatter(
            term_qkv.astype(jnp.bfloat16), "fsdp", scatter_dimension=0, tiled=True
        ).astype(jnp.float32),
        lax.psum_scatter(
            term_out.astype(jnp.bfloat16), "fsdp", scatter_dimension=1, tiled=True
        ).astype(jnp.float32),
    )
    summed_qkv, summed_out = (
        lax.psum(shard_qkv.astype(jnp.bfloat16), ("pair", "tm")).astype(jnp.float32),
        lax.psum(shard_out.astype(jnp.bfloat16), ("pair", "tm")).astype(jnp.float32),
    )
    tokens_all = (
        frames.shape[0]
        * frames.shape[1]
        * frames.shape[2]
        * lax.axis_size("pair")
        * lax.axis_size("tm")
        * lax.axis_size("fsdp")
    )
    grad_scale = 1.0 / math.sqrt(tokens_all)
    return (grad_frames, summed_qkv * grad_scale, summed_out * grad_scale)


def solution(mesh):
    return jax.shard_map(
        on_device,
        mesh=mesh,
        in_specs=(
            P("pair", "tm", "fsdp", None),
            P("pair", None),
            P("fsdp", None),
            P(None, "fsdp"),
            P("pair", "tm", "fsdp", None),
        ),
        out_specs=(P("pair", "tm", "fsdp", None), P("fsdp", None), P(None, "fsdp")),
        check_vma=False,
    )
```

profile of v0, /device:TPU:38, one launch (start us, length us, event | category | flops | bytes accessed | tf_op | source)
XLA Modules:
  0.0 570.2 jit_solution(16790569967085542983)
XLA Ops:
  7.2 0.0 all-gather.5.cloned.1.call-start
  7.2 0.7 all-gather.5.cloned.1.call-update
  7.9 0.0 all-gather.3.cloned.1.call-start
  7.9 0.7 all-gather.3.cloned.1.call-update
  8.6 1.8 fusion.15
  10.4 37.7 %all-gather.5.cloned.1.call-done = bf16[768,1536]{0,1:T(8,128)(2,1)} async-done(((bf16[768,96]{0,1:T(8,128)(2,1)}), bf16[768,1536]{0,1:T(8,128)(2,1)}) %all-gather.5.cloned.1.call-update) | async-done | bytes 2359312 | tf_op jit(solution)/shard_map/all_gather | solution.py:96
  48.2 3.5 convolution_convert_fusion.5
  51.7 0.0 copy-start
  51.7 1.3 copy.56
  53.0 7.5 %all-to-all-start.1 = ((bf16[1,8,64,768]{3,1,0,2:T(8,128)(2,1)}), bf16[1,8,64,768]{3,1,0,2:T(8,128)(2,1)S(1)}, u32[]{:S(2)}, u32[]{:S(2)}) async-start(bf16[1,8,64,768]{3,1,0,2:T(8,128)(2,1)} %copy.56), calls=%async_computation.1 | async-start | bytes 1572864 | tf_op jit(solution)/shard_map/all_to_all | solution.py:111
  60.5 0.0 copy-done
  60.5 1.5 fusion.6
  62.0 37.7 %all-gather.3.cloned.1.call-done = bf16[1536,2304]{1,0:T(8,128)(2,1)} async-done(((bf16[96,2304]{1,0:T(8,128)(2,1)}), bf16[1536,2304]{1,0:T(8,128)(2,1)}) %all-gather.3.cloned.1.call-update) | async-done | bytes 7077904 | tf_op jit(solution)/shard_map/all_gather | solution.py:95
  99.7 7.3 %convolution_convert_fusion.1 = bf16[512,2304]{1,0:T(8,128)(2,1)S(1)} fusion(bf16[512,1536]{1,0:T(8,128)(2,1)} %bitcast.92, bf16[1536,2304]{1,0:T(8,128)(2,1)} %all-gather.3.cloned.1.call-done), kind=kOutput, calls=%fused_computation.6 | convolution fusion | flops 3625058304 | bytes 11010048 | tf_op jit(solution)/shard_map/dot_general | solution.py:100
  107.0 2.7 copy.51
  109.7 0.0 all-to-all-done.1
  109.7 7.6 %all-to-all-start = ((bf16[1,8,64,2304]{3,1,0,2:T(8,128)(2,1)}), bf16[1,8,64,2304]{3,1,0,2:T(8,128)(2,1)}, u32[]{:S(2)}, u32[]{:S(2)}) async-start(bf16[1,8,64,2304]{3,1,0,2:T(8,128)(2,1)} %copy.51), calls=%async_computation | async-start | bytes 4718592 | tf_op jit(solution)/shard_map/all_to_all | solution.py:102
  117.3 0.0 copy-done.9
  117.3 0.1 broadcast_compare_fusion
  117.4 0.1 copy.103
  117.5 0.1 copy.58
  117.6 2.3 reshape.188
  119.9 3.5 copy.65
  123.4 49.7 %all-to-all-done = bf16[1,8,64,2304]{3,1,0,2:T(8,128)(2,1)} async-done(((bf16[1,8,64,2304]{3,1,0,2:T(8,128)(2,1)}), bf16[1,8,64,2304]{3,1,0,2:T(8,128)(2,1)}, u32[]{:S(2)}, u32[]{:S(2)}) %all-to-all-start) | async-done | bytes 2359328 | tf_op jit(solution)/shard_map/all_to_all | solution.py:102
  173.2 2.1 copy.102
  175.2 1.5 copy.53
  176.8 8.2 %reshape.183 = bf16[1,64,8,3,12,64]{5,4,3,2,1,0:T(8,128)(2,1)} reshape(bf16[1,8,8,8,2304]{4,3,2,1,0:T(8,128)(2,1)} %copy.53) | data formatting | bytes 4718592 | tf_op jit(solution)/shard_map/reshape | solution.py:21
  185.0 5.6 fusion.56
  190.6 2.0 fusion.45
  192.6 1.0 fusion.57
  193.6 2.4 convolution_convert_fusion.3
  196.0 0.0 copy-done.10
  196.0 2.6 copy.73
  198.6 5.6 all-to-all-start.3
  204.2 4.6 fusion.46
  208.8 8.6 %fusion.39 = bf16[1,64,8,1,12,64]{1,5,4,2,3,0:T(8,128)(2,1)} fusion(f32[8,12,64,64]{2,3,1,0:T(8,128)} %fusion.46, bf16[1,64,8,1,12,64]{5,4,3,2,1,0:T(8,128)(2,1)} %copy-done.2, f32[8,12,64,64]{2,3,1,0:T(8,128)} %copy-done.10, f32[8,12,64]{2,1,0:T(8,128)S(1)} %get-tuple-element.8), kind=kOutput, calls=%fused_computation.44 | convolution fusion | flops 53483584 | bytes 4743168 | tf_op jit(solution)/shard_map/cphij,ciphd->cjphd/dot_general | solution.py:58
  217.4 8.2 %fusion.42 = bf16[1,64,8,1,12,64]{1,5,4,2,3,0:T(8,128)(2,1)} fusion(f32[8,12,64,64]{2,3,1,0:T(8,128)} %fusion.46, bf16[1,64,8,1,12,64]{5,4,3,2,1,0:T(8,128)(2,1)} %copy-done.1, f32[8,12,64,64]{2,3,1,0:T(8,128)} %copy-done.10, f32[8,12,64]{2,1,0:T(8,128)S(1)} %get-tuple-element.8), kind=kOutput, calls=%fused_computation.45 | convolution fusion | flops 53483584 | bytes 4743168 | tf_op jit(solution)/shard_map/cphij,cjphd->ciphd/dot_general | solution.py:55
  225.6 3.0 fusion.38
  228.6 0.0 copy-done.4
  228.6 0.0 copy-done.5
  228.6 2.7 pad_maximum_fusion
  231.3 9.0 %copy.67 = bf16[1,64,8,3,12,64]{5,4,3,2,1,0:T(8,128)(2,1)} copy(bf16[1,64,8,3,12,64]{1,5,4,2,3,0:T(8,128)(2,1)} %pad_maximum_fusion) | data formatting | bytes 4718592 | tf_op jit(solution)/shard_map/stack | solution.py:64
  240.4 8.4 %reshape.190 = bf16[1,64,8,2304]{3,2,1,0:T(8,128)(2,1)} reshape(bf16[1,64,8,3,12,64]{5,4,3,2,1,0:T(8,128)(2,1)} %copy.67) | data formatting | bytes 4718592 | tf_op jit(solution)/shard_map/reshape | solution.py:65
  248.7 0.0 all-to-all-done.3
  248.8 7.4 %all-to-all-start.2 = ((bf16[1,64,8,2304]{3,2,0,1:T(8,128)(2,1)}), bf16[1,64,8,2304]{3,2,0,1:T(8,128)(2,1)}, u32[]{:S(2)}, u32[]{:S(2)}) async-start(bf16[1,64,8,2304]{3,2,0,1:T(8,128)(2,1)} %bitcast.88), calls=%async_computation.2 | async-start | bytes 4718592 | tf_op jit(solution)/shard_map/all_to_all | solution.py:113
  256.1 0.0 reduce-scatter.5.cloned.1.call-start
  256.1 1.2 copy.74
  257.3 2.9 convolution_convert_fusion.2
  260.2 0.0 reduce-scatter.5.cloned.1.call-update
  260.2 0.0 reduce-scatter.3.cloned.1.call-start
  260.3 51.2 %all-to-all-done.2 = bf16[1,64,8,2304]{3,2,0,1:T(8,128)(2,1)} async-done(((bf16[1,64,8,2304]{3,2,0,1:T(8,128)(2,1)}), bf16[1,64,8,2304]{3,2,0,1:T(8,128)(2,1)}, u32[]{:S(2)}, u32[]{:S(2)}) %all-to-all-start.2) | async-done | bytes 2359328 | tf_op jit(solution)/shard_map/all_to_all | solution.py:113
  311.5 1.8 copy.69
  313.3 6.0 %convolution_convert_fusion = bf16[1536,2304]{1,0:T(8,128)(2,1)} fusion(bf16[512,1536]{1,0:T(8,128)(2,1)S(1)} %bitcast.93, bf16[512,2304]{1,0:T(8,128)(2,1)S(1)} %bitcast.90), kind=kOutput, calls=%fused_computation.2 | convolution fusion | flops 3627417600 | bytes 11010048 | tf_op jit(solution)/shard_map/dot_general | solution.py:69
  319.3 0.0 reduce-scatter.3.cloned.1.call-update
  319.4 0.0 copy-start.8
  319.4 0.3 all-reduce.3.cloned.1.call-start
  319.7 9.4 %fusion.10 = (f32[8,64]{1,0:T(8,128)S(1)}, f32[1,8,64,1536]{3,2,1,0:T(8,128)}) fusion(bf16[1,8,64,1536]{3,2,1,0:T(8,128)(2,1)S(1)} %copy-done, f32[8,64]{1,0:T(8,128)S(1)} %add_rsqrt_fusion, bf16[1536,2304]{1,0:T(8,128)(2,1)} %all-gather.3.cloned.1.call-done, bf16[1,8,8,8,2304]{4,3,1,2,0:T(8,128)(2,1)} %bitcast.23), kind=kOutput, calls=%fused_computation.14 | convolution fusion | flops 3627023872 | bytes 14159872 | tf_op jit(solution)/shard_map/dot_general | solution.py:80
  329.1 70.9 %reduce-scatter.3.cloned.1.call-done = bf16[96,2304]{1,0:T(8,128)(2,1)} async-done(((bf16[1536,2304]{1,0:T(8,128)(2,1)}), bf16[96,2304]{1,0:T(8,128)(2,1)}) %reduce-scatter.3.cloned.1.call-update) | async-done | bytes 442384 | tf_op jit(solution)/shard_map/reduce_scatter | solution.py:118
  400.0 0.0 all-reduce.3.cloned.1.call-update
  400.0 0.0 copy-done.8
  400.0 3.9 fusion.14
  403.9 156.1 %all-reduce.3.cloned.1.call-done = (bf16[96,2304]{1,0:T(8,128)(2,1)}, bf16[768,96]{0,1:T(8,128)(2,1)}) async-done(((bf16[96,2304]{1,0:T(8,128)(2,1)}, bf16[768,96]{0,1:T(8,128)(2,1)}), (bf16[96,2304]{1,0:T(8,128)(2,1)}, bf16[768,96]{0,1:T(8,128)(2,1)})) %all-reduce.3.cloned.1.call-update) | async-done | bytes 589840 | tf_op jit(solution)/shard_map/psum | solution.py:126
  560.1 2.0 convert_multiply_fusion.2
  562.0 1.6 convert_multiply_fusion.3
  (17 shorter events, 0.0 us)
Async XLA Ops:
  7.2 41.0 %all-gather.5.cloned.1.call-start = ((), (), s32[]{:S(2)}) async-start(), calls=%async_computation.7 | async-start | bytes 2506752 | tf_op jit(solution)/shard_map/all_gather | solution.py:96
  7.9 91.8 %all-gather.3.cloned.1.call-start = ((), (), s32[]{:S(2)}) async-start(), calls=%async_computation.6 | async-start | bytes 7520256 | tf_op jit(solution)/shard_map/all_gather | solution.py:95
  51.7 8.8 %copy-start = (bf16[1,8,64,1536]{3,2,1,0:T(8,128)(2,1)S(1)}, bf16[1,8,64,1536]{3,2,1,0:T(8,128)(2,1)}, u32[]{:S(2)}) copy-start(bf16[1,8,64,1536]{3,2,1,0:T(8,128)(2,1)} %param.5) | copy-start | bytes 4718596
  53.0 56.7 %all-to-all-start.1 = ((bf16[1,8,64,768]{3,1,0,2:T(8,128)(2,1)}), bf16[1,8,64,768]{3,1,0,2:T(8,128)(2,1)S(1)}, u32[]{:S(2)}, u32[]{:S(2)}) async-start(bf16[1,8,64,768]{3,1,0,2:T(8,128)(2,1)} %copy.56), calls=%async_computation.1 | async-start | bytes 1572864 | tf_op jit(solution)/shard_map/all_to_all | solution.py:111
  109.7 7.6 %copy-start.9 = (s32[1,64]{1,0:T(1,128)S(1)}, s32[1,64]{1,0:T(1,128)}, u32[]{:S(2)}) copy-start(s32[1,64]{1,0:T(1,128)} %param.6) | copy-start | bytes 772
  109.7 63.5 %all-to-all-start = ((bf16[1,8,64,2304]{3,1,0,2:T(8,128)(2,1)}), bf16[1,8,64,2304]{3,1,0,2:T(8,128)(2,1)}, u32[]{:S(2)}, u32[]{:S(2)}) async-start(bf16[1,8,64,2304]{3,1,0,2:T(8,128)(2,1)} %copy.51), calls=%async_computation | async-start | bytes 4718592 | tf_op jit(solution)/shard_map/all_to_all | solution.py:102
  190.6 2.0 copy-start.1
  190.6 2.0 copy-start.2
  190.6 3.0 copy-start.3
  193.6 2.5 copy-start.10
  198.6 50.2 %all-to-all-start.3 = ((bf16[1,64,8,768]{3,2,0,1:T(8,128)(2,1)}), bf16[1,64,8,768]{3,2,0,1:T(8,128)(2,1)}, u32[]{:S(2)}, u32[]{:S(2)}) async-start(bf16[1,64,8,768]{3,2,0,1:T(8,128)(2,1)} %copy.73), calls=%async_computation.4 | async-start | bytes 1572864 | tf_op jit(solution)/shard_map/all_to_all | solution.py:104
  225.6 3.0 copy-start.4
  225.6 3.0 copy-start.5
  248.8 8.6 %copy-start.7 = (bf16[1,8,64,1536]{3,2,1,0:T(8,128)(2,1)S(1)}, bf16[1,8,64,1536]{3,2,1,0:T(8,128)(2,1)}, u32[]{:S(2)}) copy-start(bf16[1,8,64,1536]{3,2,1,0:T(8,128)(2,1)} %param.9) | copy-start | bytes 4718596
  248.8 62.7 %all-to-all-start.2 = ((bf16[1,64,8,2304]{3,2,0,1:T(8,128)(2,1)}), bf16[1,64,8,2304]{3,2,0,1:T(8,128)(2,1)}, u32[]{:S(2)}, u32[]{:S(2)}) async-start(bf16[1,64,8,2304]{3,2,0,1:T(8,128)(2,1)} %bitcast.88), calls=%async_computation.2 | async-start | bytes 4718592 | tf_op jit(solution)/shard_map/all_to_all | solution.py:113
  256.1 73.0 %reduce-scatter.5.cloned.1.call-start = ((), (), s32[]{:S(2)}) async-start(), calls=%async_computation.9 | async-start | bytes 2506752 | tf_op jit(solution)/shard_map/reduce_scatter | solution.py:121
  260.2 53.1 %copy-start.6 = (bf16[1,8,64,1536]{3,2,1,0:T(8,128)(2,1)S(1)}, bf16[1,8,64,1536]{3,2,1,0:T(8,128)(2,1)}, u32[]{:S(2)}) copy-start(bf16[1,8,64,1536]{3,2,1,0:T(8,128)(2,1)} %fusion.6) | copy-start | bytes 4718596
  260.2 139.8 %reduce-scatter.3.cloned.1.call-start = ((), (), s32[]{:S(2)}) async-start(), calls=%async_computation.8 | async-start | bytes 7520256 | tf_op jit(solution)/shard_map/reduce_scatter | solution.py:118
  319.4 80.7 %copy-start.8 = (bf16[1,8,64,1536]{3,2,1,0:T(8,128)(2,1)S(1)}, bf16[1,8,64,1536]{3,2,1,0:T(8,128)(2,1)}, u32[]{:S(2)}) copy-start(bf16[1,8,64,1536]{3,2,1,0:T(8,128)(2,1)} %param.9) | copy-start | bytes 4718596
  319.4 240.7 %all-reduce.3.cloned.1.call-start = ((), (), s32[]{:S(2)}) async-start(), calls=%async_computation.10 | async-start | bytes 1179648 | tf_op jit(solution)/shard_map/psum | solution.py:126
Sparse Core Ops, SparseCore 0:
  9.8 38.2 all-gather.4
  50.0 49.6 all-gather.2
  260.4 64.1 reduce-scatter.4
  327.0 72.9 reduce-scatter.2
  402.8 157.2 all-reduce.2
where the time goes:
time: 575 us; the launch traced here: 570 us
  waiting for transfers between devices  405 us (70%)
  matrix products  57.9 us (10%)
  local copies, waits for them, and re-layouts  50.5 us (9%)
  starting transfers between devices  28.5 us (5%)
  other arithmetic  14.6 us (3%)
  between operations  14 us (2%)
    psum x1, waiting for transfers between devices, on_device(): lax.psum(shard_qkv.astype(jnp.bfloat16), ('pair', 'tm')).astype(jnp.float32)  156 us
    reduce_scatter x1, waiting for transfers between devices, on_device(): lax.psum_scatter(term_qkv.astype(jnp.bfloat16), 'fsdp', scatter_dimension...  70.9 us
    all_to_all x1, waiting for transfers between devices, on_device(): lax.all_to_all(d_qkv_here, 'tm', split_axis=1, concat_axis=2, tiled=True)  51.2 us
    all_to_all x1, waiting for transfers between devices, on_device(): lax.all_to_all(qkv, 'tm', split_axis=2, concat_axis=1, tiled=True)  49.7 us
    all_gather x1, waiting for transfers between devices, on_device(): lax.all_gather(w_out, 'fsdp', axis=1, tiled=True)  37.7 us
    all_gather x1, waiting for transfers between devices, on_device(): lax.all_gather(w_qkv, 'fsdp', axis=0, tiled=True)  37.7 us
  transfers between devices with their start and end apart: 9, of which 6 were waited for; matrix products, arithmetic and copies ran while one was open for 16% of the time, Pallas kernels for 0%

commit v1 on v0

v1 whole, which is shorter than its diff:
```python
import math

import jax
import jax.numpy as jnp
import numpy as np
from jax import lax
from jax.experimental import pallas as pl
from jax.experimental.pallas import tpu as pltpu
from jax.sharding import Mesh
from jax.sharding import PartitionSpec as P

HEAD_DIM = 64
FSDP = ("yl", "x", "core")
GROUP = ("pair", "tm")
MASKED = -1e30
VMEM_BYTES = 48 * 1024 * 1024


def low_half(rows):
    return lax.broadcasted_iota(jnp.int32, (rows, 2 * HEAD_DIM), 1) < HEAD_DIM


def stack_heads(pair_rows):
    first = low_half(pair_rows.shape[0])
    zero = jnp.zeros_like(pair_rows)
    return jnp.concatenate([jnp.where(first, pair_rows, zero), jnp.where(first, zero, pair_rows)], axis=0)


def merge_heads(stacked):
    rows = stacked.shape[0] // 2
    return jnp.where(low_half(rows), stacked[:rows], stacked[rows:])


def contract(left, right, left_dim, right_dim):
    return lax.dot_general(
        left, right, (((left_dim,), (right_dim,)), ((), ())), preferred_element_type=jnp.float32
    )


def forward_kernel(mask_ref, qkv_ref, mixed_ref, weights_ref):
    wide = 2 * HEAD_DIM
    inner = mixed_ref.shape[-1]
    rows = mask_ref.shape[1]
    allowed = mask_ref[...] > 0.5
    for pair in range(inner // wide):
        first = pair * wide
        queries = stack_heads(qkv_ref[..., first : first + wide].reshape(rows, wide))
        keys = qkv_ref[..., inner + first : inner + first + wide].reshape(rows, wide)
        values = qkv_ref[..., 2 * inner + first : 2 * inner + first + wide].reshape(rows, wide)
        scores = contract(queries, keys, 1, 1) * HEAD_DIM ** (-0.5)
        scores = jnp.where(allowed, scores, MASKED)
        exponent = jnp.exp(scores - jnp.max(scores, axis=-1, keepdims=True))
        weights = exponent / jnp.sum(exponent, axis=-1, keepdims=True)
        weights_ref[0, pair] = weights
        mixed = merge_heads(contract(weights.astype(jnp.bfloat16), values, 1, 0))
        mixed_ref[..., first : first + wide] = mixed.astype(jnp.bfloat16).reshape(
            mixed_ref.shape[:-1] + (wide,)
        )


def backward_kernel(qkv_ref, d_mixed_ref, weights_ref, d_qkv_ref):
    wide = 2 * HEAD_DIM
    inner = d_mixed_ref.shape[-1]
    rows = weights_ref.shape[-1]
    block = d_mixed_ref.shape[:-1] + (wide,)
    for pair in range(inner // wide):
        first = pair * wide
        queries = stack_heads(qkv_ref[..., first : first + wide].reshape(rows, wide))
        keys = qkv_ref[..., inner + first : inner + first + wide].reshape(rows, wide)
        values = qkv_ref[..., 2 * inner + first : 2 * inner + first + wide].reshape(rows, wide)
        d_heads = stack_heads(d_mixed_ref[..., first : first + wide].reshape(rows, wide))
        weights = weights_ref[0, pair]
        d_weights = contract(d_heads, values, 1, 1)
        centered = d_weights - jnp.sum(weights * d_weights, axis=-1, keepdims=True)
        d_scores = (weights * centered * HEAD_DIM ** (-0.5)).astype(jnp.bfloat16)
        d_query = merge_heads(contract(d_scores, keys, 1, 0))
        d_key = contract(d_scores, queries, 0, 0)
        d_value = contract(weights.astype(jnp.bfloat16), d_heads, 0, 0)
        for place, value in enumerate((d_query, d_key, d_value)):
            start = place * inner + first
            d_qkv_ref[..., start : start + wide] = value.astype(jnp.bfloat16).reshape(block)


def attention_forward(qkv, mask, inner):
    senders, patches, frames_each, triple = qkv.shape
    groups = patches // 2
    rows = senders * 2 * frames_each
    pairs = inner // (2 * HEAD_DIM)
    return pl.pallas_call(
        forward_kernel,
        grid=(groups,),
        in_specs=[
            pl.BlockSpec((2 * rows, rows), lambda g: (0, 0)),
            pl.BlockSpec((senders, 2, frames_each, triple), lambda g: (0, g, 0, 0)),
        ],
        out_specs=[
            pl.BlockSpec((senders, 2, frames_each, inner), lambda g: (0, g, 0, 0)),
            pl.BlockSpec((1, pairs, 2 * rows, rows), lambda g: (g, 0, 0, 0)),
        ],
        out_shape=[
            jax.ShapeDtypeStruct((senders, patches, frames_each, inner), jnp.bfloat16),
            jax.ShapeDtypeStruct((groups, pairs, 2 * rows, rows), jnp.float32),
        ],
        compiler_params=pltpu.CompilerParams(vmem_limit_bytes=VMEM_BYTES),
        cost_estimate=pl.CostEstimate(
            flops=groups * pairs * 2 * 2 * rows * rows * 256,
            bytes_accessed=8 * 1024 * 1024,
            transcendentals=groups * pairs * 2 * rows * rows,
        ),
    )(mask, qkv)


def attention_backward(qkv, d_mixed, weights):
    senders, patches, frames_each, inner = d_mixed.shape
    groups, pairs, double_rows, rows = weights.shape
    return pl.pallas_call(
        backward_kernel,
        grid=(groups,),
        in_specs=[
            pl.BlockSpec((senders, 2, frames_each, 3 * inner), lambda g: (0, g, 0, 0)),
            pl.BlockSpec((senders, 2, frames_each, inner), lambda g: (0, g, 0, 0)),
            pl.BlockSpec((1, pairs, double_rows, rows), lambda g: (g, 0, 0, 0)),
        ],
        out_specs=pl.BlockSpec((senders, 2, frames_each, 3 * inner), lambda g: (0, g, 0, 0)),
        out_shape=jax.ShapeDtypeStruct((senders, patches, frames_each, 3 * inner), jnp.bfloat16),
        compiler_params=pltpu.CompilerParams(vmem_limit_bytes=VMEM_BYTES),
        cost_estimate=pl.CostEstimate(
            flops=groups * pairs * 4 * 2 * rows * rows * 256,
            bytes_accessed=10 * 1024 * 1024,
            transcendentals=0,
        ),
    )(qkv, d_mixed, weights)


def to_patch_owner(block):
    frames_each, patches_here, width = block.shape[1:]
    owners = lax.axis_size("tm")
    split = block.reshape(frames_each, owners, patches_here // owners, width)
    return lax.all_to_all(
        split.transpose(1, 2, 0, 3), "tm", split_axis=0, concat_axis=0, tiled=True
    )


def to_frame_owner(block):
    owners, patches_each, frames_each, width = block.shape
    back = lax.all_to_all(block, "tm", split_axis=0, concat_axis=0, tiled=True)
    return back.transpose(2, 0, 1, 3).reshape(1, frames_each, owners * patches_each, width)


def attention_mask(frame_time, senders, frames_each):
    rows = np.arange(senders * 2 * frames_each)
    patch = (rows // frames_each) % 2
    frame = (rows // (2 * frames_each)) * frames_each + rows % frames_each
    times = frame_time[0][frame]
    allowed = (times[None, :] <= times[:, None]) & (patch[None, :] == patch[:, None])
    allowed = allowed.astype(jnp.float32)
    return jnp.concatenate([allowed, allowed], axis=0)


def sum_over_group(shard):
    rows, width = shard.shape
    pairs, times = lax.axis_size("pair"), lax.axis_size("tm")
    parts = shard.reshape(pairs, rows // pairs, times, width // times).transpose(0, 2, 1, 3)
    parts = parts.reshape(pairs * times, rows // pairs, width // times)
    received = lax.all_to_all(parts, GROUP, split_axis=0, concat_axis=0, tiled=True)
    mine = jnp.sum(received.astype(jnp.float32), axis=0).astype(jnp.bfloat16)
    spread = jnp.broadcast_to(mine[None], parts.shape)
    whole = lax.all_to_all(spread, GROUP, split_axis=0, concat_axis=0, tiled=True)
    whole = whole.reshape(pairs, times, rows // pairs, width // times).transpose(0, 2, 1, 3)
    return whole.reshape(rows, width)


def on_device(frames, frame_time, w_qkv, w_out, grad_out):
    inner = w_out.shape[0]
    width = frames.shape[-1]
    gathered = lax.all_gather(
        jnp.concatenate([w_qkv, w_out.T], axis=1), FSDP, axis=0, tiled=True
    )
    full_qkv = gathered[:, : 3 * inner]
    full_out_t = gathered[:, 3 * inner :]
    tokens = to_patch_owner(frames)
    grad_tokens = to_patch_owner(grad_out)
    token_shape = tokens.shape
    senders, patches_each, frames_each = token_shape[:3]
    mask = attention_mask(frame_time, senders, frames_each)

    float_rows = tokens.reshape(-1, width).astype(jnp.float32)
    inv_rms = lax.rsqrt(jnp.mean(float_rows * float_rows, axis=-1, keepdims=True) + 1e-06)
    normed = (float_rows * inv_rms).astype(jnp.bfloat16)
    qkv = jnp.dot(normed, full_qkv, preferred_element_type=jnp.float32).astype(jnp.bfloat16)
    qkv = qkv.reshape(token_shape[:3] + (3 * inner,))
    mixed, weights = attention_forward(qkv, mask, inner)

    grad_rows = grad_tokens.reshape(-1, width)
    d_mixed = jnp.dot(grad_rows, full_out_t, preferred_element_type=jnp.float32).astype(jnp.bfloat16)
    d_qkv = attention_backward(qkv, d_mixed.reshape(token_shape[:3] + (inner,)), weights)
    d_rows = d_qkv.reshape(-1, 3 * inner)

    term = jnp.concatenate(
        [
            contract(normed, d_rows, 0, 0).astype(jnp.bfloat16),
            contract(grad_rows, mixed.reshape(-1, inner), 0, 0).astype(jnp.bfloat16),
        ],
        axis=1,
    )
    shard = lax.psum_scatter(term, FSDP, scatter_dimension=0, tiled=True)

    d_normed = contract(d_rows, full_qkv, 1, 1)
    scaled = float_rows * inv_rms
    inner_term = jnp.mean(d_normed * scaled, axis=-1, keepdims=True)
    grad_local = grad_rows.astype(jnp.float32) + inv_rms * (d_normed - scaled * inner_term)
    grad_frames = to_frame_owner(grad_local.astype(jnp.bfloat16).reshape(token_shape))

    summed = sum_over_group(shard).astype(jnp.float32)
    tokens_all = frames.shape[0] * frames.shape[1] * frames.shape[2]
    for axis in GROUP + FSDP:
        tokens_all *= lax.axis_size(axis)
    scaled_sum = summed * (1.0 / math.sqrt(tokens_all))
    return (grad_frames, scaled_sum[:, : 3 * inner], scaled_sum[:, 3 * inner :].T)


def solution(mesh):
    pairs, times, shards = (mesh.shape[name] for name in ("pair", "tm", "fsdp"))
    cut = Mesh(
        mesh.devices.reshape(pairs, times, 2, shards // 4, 2), ("pair", "tm") + FSDP
    )
    tokens_spec = P("pair", "tm", FSDP, None)
    return jax.shard_map(
        on_device,
        mesh=cut,
        in_specs=(tokens_spec, P("pair", None), P(FSDP, None), P(None, FSDP), tokens_spec),
        out_specs=(tokens_spec, P(FSDP, None), P(None, FSDP)),
        check_vma=False,
    )
```

time: 575 us -> 308 us (0.54)
  waiting for transfers between devices: 405 us -> 191 us
  local copies, waits for them, and re-layouts: 50.5 us -> 12.2 us
  matrix products: 57.9 us -> 27.9 us
  Pallas kernels: 0 us -> 14.7 us
  starting transfers between devices: 28.5 us -> 35.1 us
    psum x1 -> x0, waiting for transfers between devices: 156 us -> none  [on_device(): lax.psum(shard_qkv.astype(jnp.bfloat16), ('pair', 'tm')).astype(jnp.float32)]
    all_gather x2 -> x1, waiting for transfers between devices: 75.4 us -> 4.96 us  [on_device(): lax.all_gather(jnp.concatenate([w_qkv, w_out.T], axis=1), FSDP, axis=0, t...]
    dot_general x11 -> x5, matrix products: 57.9 us -> 27.9 us  [the longest x3 17 us: contract(): lax.dot_general(left, right, (((left_dim,), (right_dim,)), ((), ())), pre...]
    reshape x5 -> x2, local copies, waits for them, and re-layouts: 23.2 us -> 2.9 us  [the longest x1 2.01 us: to_patch_owner(): split = block.reshape(frames_each, owners, patches_here // owners, width)]
    another operation x3 -> x0, local copies, waits for them, and re-layouts: 14.9 us -> none  [the longest x1 9.04 us: attention_backward(): stacked = jnp.stack([d_query, d_key, d_value], axis=3)]
    pallas_call x0 -> x2, Pallas kernels: none -> 14.7 us  [the longest x1 9.5 us: attention_backward(): pl.pallas_call(backward_kernel, grid=(groups,), in_specs=[pl.BlockSpec((s...]
    all_to_all x4 -> x5, waiting for transfers between devices: 101 us -> 114 us  [the longest x2 52.5 us: to_patch_owner(): lax.all_to_all(split.transpose(1, 2, 0, 3), 'tm', split_axis=0, concat_ax...]
    all_to_all x4 -> x5, starting transfers between devices: 28 us -> 35 us  [the longest x2 14.4 us: to_patch_owner(): lax.all_to_all(split.transpose(1, 2, 0, 3), 'tm', split_axis=0, concat_ax...]
  transfers between devices with their start and end apart: 9 -> 7, of which waited for: 6 -> 7; matrix products, arithmetic and copies ran while one was open for 16% -> 9% of each run, Pallas kernels for 0% -> 2%
where the time goes in v1:
time: 308 us; the launch traced here: 307 us
  waiting for transfers between devices  191 us (62%)
  starting transfers between devices  35.1 us (11%)
  matrix products  27.9 us (9%)
  Pallas kernels  14.7 us (5%)
  between operations  14.3 us (5%)
  other arithmetic  12.3 us (4%)
  local copies, waits for them, and re-layouts  12.2 us (4%)
    reduce_scatter x1, waiting for transfers between devices, on_device(): shard = lax.psum_scatter(term, FSDP, scatter_dimension=0, tiled=True)  72 us
    all_to_all x2, waiting for transfers between devices, to_patch_owner(): lax.all_to_all(split.transpose(1, 2, 0, 3), 'tm', split_axis=0, concat_ax...  52.5 us
    all_to_all x1, waiting for transfers between devices, to_frame_owner(): back = lax.all_to_all(block, 'tm', split_axis=0, concat_axis=0, tiled=True)  39.5 us
    dot_general x3, matrix products, contract(): lax.dot_general(left, right, (((left_dim,), (right_dim,)), ((), ())), pre...  17 us
    all_to_all x1, waiting for transfers between devices, sum_over_group(): lax.all_to_all(spread, GROUP, split_axis=0, concat_axis=0, tiled=True)  15.5 us
    all_to_all x2, starting transfers between devices, to_patch_owner(): lax.all_to_all(split.transpose(1, 2, 0, 3), 'tm', split_axis=0, concat_ax...  14.4 us
    all_to_all x1, starting transfers between devices, sum_over_group(): lax.all_to_all(parts, GROUP, split_axis=0, concat_axis=0, tiled=True)  9.94 us
    pallas_call x1, Pallas kernels, attention_backward(): pl.pallas_call(backward_kernel, grid=(groups,), in_specs=[pl.BlockSpec((s...  9.5 us
  transfers between devices with their start and end apart: 7, of which 7 were waited for; matrix products, arithmetic and copies ran while one was open for 9% of the time, Pallas kernels for 2%

profile of v1, /device:TPU:38, one launch (start us, length us, event | category | flops | bytes accessed | tf_op | source)
XLA Modules:
  0.0 307.1 jit_solution(7660801836682916908)
XLA Ops:
  7.2 0.0 copy-start
  7.2 0.0 copy-start.7
  7.2 0.0 all-gather.2.cloned.1.call-start
  7.2 2.1 pad_maximum_fusion.1
  9.3 0.0 all-gather.2.cloned.1.call-update
  9.3 0.0 copy-done.7
  9.3 2.0 copy.34
  11.3 8.7 %all-to-all-start.1 = ((bf16[8,8,8,1536]{3,2,1,0:T(8,128)(2,1)}), bf16[8,8,8,1536]{3,2,1,0:T(8,128)(2,1)S(1)}, u32[]{:S(2)}, u32[]{:S(2)}) async-start(bf16[8,8,8,1536]{3,2,1,0:T(8,128)(2,1)} %bitcast.58), calls=%async_computation.1 | async-start | bytes 3145728 | tf_op jit(solution)/shard_map/all_to_all | solution.py:139
  20.0 0.0 copy-done.8
  20.0 2.1 copy.20
  22.1 36.4 %all-to-all-done.1 = bf16[8,8,8,1536]{3,2,1,0:T(8,128)(2,1)S(1)} async-done(((bf16[8,8,8,1536]{3,2,1,0:T(8,128)(2,1)}), bf16[8,8,8,1536]{3,2,1,0:T(8,128)(2,1)S(1)}, u32[]{:S(2)}, u32[]{:S(2)}) %all-to-all-start.1) | async-done | bytes 1572896 | tf_op jit(solution)/shard_map/all_to_all | solution.py:139
  58.6 5.7 %all-to-all-start = ((bf16[8,8,8,1536]{3,2,1,0:T(8,128)(2,1)}), bf16[8,8,8,1536]{3,2,1,0:T(8,128)(2,1)}, u32[]{:S(2)}, u32[]{:S(2)}) async-start(bf16[8,8,8,1536]{3,2,1,0:T(8,128)(2,1)} %bitcast.1), calls=%async_computation | async-start | bytes 3145728 | tf_op jit(solution)/shard_map/all_to_all | solution.py:139
  64.2 0.0 reduce-scatter.2.cloned.1.call-start
  64.2 0.0 copy-done.12
  64.2 0.0 copy-done
  64.2 1.2 gather_fusion
  65.5 0.0 copy-done.11
  65.5 0.1 compare_and_fusion
  65.6 0.4 multiply_reduce_fusion.1
  66.0 0.1 rsqrt.13
  66.1 0.0 copy-done.3
  66.1 0.0 copy-start.9
  66.1 1.5 fusion.8
  67.6 0.0 copy-done.9
  67.6 5.0 %all-gather.2.cloned.1.call-done = bf16[1536,3072]{1,0:T(8,128)(2,1)} async-done(((bf16[96,3072]{1,0:T(8,128)(2,1)}), bf16[1536,3072]{1,0:T(8,128)(2,1)}) %all-gather.2.cloned.1.call-update) | async-done | bytes 9437200 | tf_op jit(solution)/shard_map/all_gather | solution.py:176
  72.5 7.3 %fusion.4 = bf16[512,2304]{1,0:T(8,128)(2,1)S(1)} fusion(bf16[512,1536]{1,0:T(8,128)(2,1)} %fusion.8, bf16[1536,3072]{1,0:T(8,128)(2,1)} %all-gather.2.cloned.1.call-done), kind=kOutput, calls=%fused_computation.8 | convolution fusion | flops 3625058304 | bytes 11010048 | tf_op jit(solution)/shard_map/dot_general | solution.py:190
  79.8 5.2 %shard_map.103 = (bf16[8,8,8,768]{3,2,1,0:T(8,128)(2,1)S(1)}, f32[4,6,256,128]{3,2,1,0:T(8,128)}) custom-call(f32[256,128]{1,0:T(8,128)S(1)} %add_convert_fusion.1.mask_ref, bf16[8,8,8,2304]{3,2,1,0:T(8,128)(2,1)S(1)} %bitcast.60), custom_call_target="tpu_custom_call" | custom-call | flops 402653184 | bytes 8388608 | tf_op jit(solution)/shard_map/pallas_call | solution.py:89
  85.1 16.0 %all-to-all-done = bf16[8,8,8,1536]{3,2,1,0:T(8,128)(2,1)} async-done(((bf16[8,8,8,1536]{3,2,1,0:T(8,128)(2,1)}), bf16[8,8,8,1536]{3,2,1,0:T(8,128)(2,1)}, u32[]{:S(2)}, u32[]{:S(2)}) %all-to-all-start) | async-done | bytes 1572896 | tf_op jit(solution)/shard_map/all_to_all | solution.py:139
  101.1 3.6 %fusion.12 = bf16[768,512]{0,1:T(8,128)(2,1)S(1)} fusion(bf16[512,1536]{1,0:T(8,128)(2,1)} %bitcast.2, bf16[1536,3072]{1,0:T(8,128)(2,1)} %all-gather.2.cloned.1.call-done), kind=kOutput, calls=%fused_computation.21 | convolution fusion | flops 1208352768 | bytes 4718592 | tf_op jit(solution)/shard_map/dot_general | solution.py:195
  104.8 9.5 %shard_map.104 = bf16[8,8,8,2304]{3,2,1,0:T(8,128)(2,1)S(1)} custom-call(bf16[8,8,8,2304]{3,2,1,0:T(8,128)(2,1)S(1)} %bitcast.61, bf16[8,8,8,768]{3,2,1,0:T(8,128)(2,1)S(1)} %bitcast.63, f32[4,6,256,128]{3,2,1,0:T(8,128)} %get-tuple-element.5.weights_ref), custom_call_target="tpu_custom_call" | custom-call | flops 805306368 | bytes 10485760 | tf_op jit(solution)/shard_map/pallas_call | solution.py:116
  114.3 0.0 copy-start.1
  114.3 0.0 copy-start.4
  114.3 5.1 %fusion.7 = bf16[1536,768]{1,0:T(8,128)(2,1)} fusion(bf16[8,8,8,768]{3,2,1,0:T(8,128)(2,1)S(1)} %get-tuple-element.6, bf16[8,8,8,1536]{3,2,1,0:T(8,128)(2,1)} %all-to-all-done), kind=kOutput, calls=%fused_computation.14 | convolution fusion | flops 1209139200 | bytes 4718592 | tf_op jit(solution)/shard_map/dot_general | solution.py:35
  119.4 0.0 copy-done.1
  119.4 0.0 copy-done.4
  119.4 4.4 %bitcast_convert_fusion = bf16[1536,2304]{1,0:T(8,128)(2,1)S(1)} fusion(bf16[8,8,8,2304]{3,2,1,0:T(8,128)(2,1)S(1)} %shard_map.104, bf16[8,8,8,1536]{3,2,1,0:T(8,128)(2,1)S(1)} %copy-done.4, f32[8,8,8]{2,1,0:T(8,128)S(1)} %add_rsqrt_fusion), kind=kOutput, calls=%fused_computation.1 | convolution fusion | flops 3629776896 | bytes 11012096 | tf_op jit(solution)/shard_map/dot_general | solution.py:35
  123.8 0.0 copy-done.6
  123.8 4.6 %pad_maximum_fusion = bf16[1536,3072]{1,0:T(8,128)(2,1)} fusion(bf16[1536,768]{1,0:T(8,128)(2,1)S(1)} %copy-done.6, bf16[1536,2304]{1,0:T(8,128)(2,1)S(1)} %bitcast_convert_fusion), kind=kLoop, calls=%fused_computation.2 | loop fusion | flops 18874368 | bytes 18874368 | tf_op jit(solution)/shard_map/concatenate | solution.py:199
  128.4 0.0 reduce-scatter.2.cloned.1.call-update
  128.4 0.0 copy-start.2
  128.5 0.0 copy-start.10
  128.5 72.0 %reduce-scatter.2.cloned.1.call-done = bf16[96,3072]{1,0:T(8,128)(2,1)} async-done(((bf16[1536,3072]{1,0:T(8,128)(2,1)}), bf16[96,3072]{1,0:T(8,128)(2,1)}) %reduce-scatter.2.cloned.1.call-update) | async-done | bytes 589840 | tf_op jit(solution)/shard_map/reduce_scatter | solution.py:206
  200.5 1.1 copy.29
  201.6 0.9 copy.24
  202.5 9.9 %all-to-all-start.3 = ((bf16[16,48,384]{2,1,0:T(8,128)(2,1)}), bf16[16,48,384]{2,1,0:T(8,128)(2,1)S(1)}, u32[]{:S(2)}, u32[]{:S(2)}) async-start(bf16[16,48,384]{2,1,0:T(8,128)(2,1)} %bitcast.20), calls=%async_computation.4 | async-start | bytes 1179648 | tf_op jit(solution)/shard_map/all_to_all | solution.py:165
  212.5 0.0 copy-done.2
  212.5 0.0 copy-done.10
  212.5 0.0 copy-start.5
  212.5 7.5 %multiply_reduce_fusion = (f32[512]{0:T(512)S(1)}, f32[512,1536]{1,0:T(8,128)S(1)}) fusion(bf16[8,8,8,1536]{3,2,1,0:T(8,128)(2,1)} %copy-done.3, f32[512]{0:T(512)S(1)} %copy-done.10, bf16[512,2304]{1,0:T(8,128)(2,1)S(1)} %bitcast.62, bf16[1536,3072]{1,0:T(8,128)(2,1)} %all-gather.2.cloned.1.call-done), kind=kOutput, calls=%fused_computation.12 | convolution fusion | flops 3627023872 | bytes 14159872 | tf_op jit(solution)/shard_map/dot_general | solution.py:35
  220.0 0.0 copy-done.5
  220.0 3.5 %add_convert_fusion = bf16[512,1536]{1,0:T(8,128)(2,1)} fusion(f32[512,1536]{1,0:T(8,128)S(1)} %get-tuple-element.8, bf16[8,8,8,1536]{3,2,1,0:T(8,128)(2,1)S(1)} %copy-done.5, f32[512]{0:T(512)S(1)} %broadcast_multiply_fusion, f32[512]{0:T(512)S(1)} %copy-done.10, bf16[8,8,8,1536]{3,2,1,0:T(8,128)(2,1)} %all-to-all-done), kind=kLoop, calls=%fused_computation.11 | loop fusion | flops 6291456 | bytes 7868416 | tf_op jit(solution)/shard_map/convert_element_type | solution.py:212
  223.4 6.1 %all-to-all-done.3 = bf16[16,48,384]{2,1,0:T(8,128)(2,1)S(1)} async-done(((bf16[16,48,384]{2,1,0:T(8,128)(2,1)}), bf16[16,48,384]{2,1,0:T(8,128)(2,1)S(1)}, u32[]{:S(2)}, u32[]{:S(2)}) %all-to-all-start.3) | async-done | bytes 589856 | tf_op jit(solution)/shard_map/all_to_all | solution.py:165
  229.6 5.8 %all-to-all-start.2 = ((bf16[8,8,8,1536]{3,2,1,0:T(8,128)(2,1)}), bf16[8,8,8,1536]{3,2,1,0:T(8,128)(2,1)S(1)}, u32[]{:S(2)}, u32[]{:S(2)}) async-start(bf16[8,8,8,1536]{3,2,1,0:T(8,128)(2,1)} %bitcast.12), calls=%async_computation.2 | async-start | bytes 3145728 | tf_op jit(solution)/shard_map/all_to_all | solution.py:146
  235.4 0.1 reduce_sum.32
  235.5 39.5 %all-to-all-done.2 = bf16[8,8,8,1536]{3,2,1,0:T(8,128)(2,1)S(1)} async-done(((bf16[8,8,8,1536]{3,2,1,0:T(8,128)(2,1)}), bf16[8,8,8,1536]{3,2,1,0:T(8,128)(2,1)S(1)}, u32[]{:S(2)}, u32[]{:S(2)}) %all-to-all-start.2) | async-done | bytes 1572896 | tf_op jit(solution)/shard_map/all_to_all | solution.py:146
  275.0 0.9 broadcast_in_dim.5
  275.9 4.9 %all-to-all-start.4 = ((bf16[16,48,384]{2,1,0:T(8,128)(2,1)}), bf16[16,48,384]{2,1,0:T(8,128)(2,1)S(1)}, u32[]{:S(2)}, u32[]{:S(2)}) async-start(bf16[16,48,384]{2,1,0:T(8,128)(2,1)} %broadcast_in_dim.5), calls=%async_computation.5 | async-start | bytes 1179648 | tf_op jit(solution)/shard_map/all_to_all | solution.py:168
  280.8 1.6 copy.33
  282.4 15.5 %all-to-all-done.4 = bf16[16,48,384]{2,1,0:T(8,128)(2,1)S(1)} async-done(((bf16[16,48,384]{2,1,0:T(8,128)(2,1)}), bf16[16,48,384]{2,1,0:T(8,128)(2,1)S(1)}, u32[]{:S(2)}, u32[]{:S(2)}) %all-to-all-start.4) | async-done | bytes 589856 | tf_op jit(solution)/shard_map/all_to_all | solution.py:168
  297.9 0.1 convert_multiply_fusion
  298.0 0.4 copy.25
  298.3 0.2 copy.30
  298.6 0.7 slice_bitcast_fusion
  299.3 1.0 slice.20
  (9 shorter events, 0.0 us)
Async XLA Ops:
  7.2 57.1 %copy-start = (s32[1,64]{1,0:T(1,128)S(1)}, s32[1,64]{1,0:T(1,128)}, u32[]{:S(2)}) copy-start(s32[1,64]{1,0:T(1,128)} %param.9) | copy-start | bytes 772
  7.2 2.1 copy-start.7
  7.2 65.3 %all-gather.2.cloned.1.call-start = ((), (), s32[]{:S(2)}) async-start(), calls=%async_computation.6 | async-start | bytes 10027008 | tf_op jit(solution)/shard_map/all_gather | solution.py:176
  11.3 8.7 %copy-start.8 = (bf16[1,8,64,1536]{3,2,1,0:T(8,128)(2,1)S(1)}, bf16[1,8,64,1536]{3,2,1,0:T(8,128)(2,1)}, u32[]{:S(2)}) copy-start(bf16[1,8,64,1536]{3,2,1,0:T(8,128)(2,1)} %param.12) | copy-start | bytes 4718596
  11.3 47.2 %all-to-all-start.1 = ((bf16[8,8,8,1536]{3,2,1,0:T(8,128)(2,1)}), bf16[8,8,8,1536]{3,2,1,0:T(8,128)(2,1)S(1)}, u32[]{:S(2)}, u32[]{:S(2)}) async-start(bf16[8,8,8,1536]{3,2,1,0:T(8,128)(2,1)} %bitcast.58), calls=%async_computation.1 | async-start | bytes 3145728 | tf_op jit(solution)/shard_map/all_to_all | solution.py:139
  22.1 42.1 %copy-start.12 = (s32[128]{0:T(128)S(1)}, s32[128]{0:T(128)}, u32[]{:S(2)}) copy-start(s32[128]{0:T(128)} %constant.27) | copy-start | bytes 1540
  22.1 43.4 %copy-start.11 = (pred[128,128]{1,0:T(32,128)(4,1)S(1)}, pred[128,128]{1,0:T(32,128)(4,1)}, u32[]{:S(2)}) copy-start(pred[128,128]{1,0:T(32,128)(4,1)} %constant.22.clone) | copy-start | bytes 49156
  58.6 7.5 %copy-start.3 = (bf16[8,8,8,1536]{3,2,1,0:T(8,128)(2,1)}, bf16[8,8,8,1536]{3,2,1,0:T(8,128)(2,1)S(1)}, u32[]{:S(2)}) copy-start(bf16[8,8,8,1536]{3,2,1,0:T(8,128)(2,1)S(1)} %all-to-all-done.1) | copy-start | bytes 4718596
  58.6 42.6 %all-to-all-start = ((bf16[8,8,8,1536]{3,2,1,0:T(8,128)(2,1)}), bf16[8,8,8,1536]{3,2,1,0:T(8,128)(2,1)}, u32[]{:S(2)}, u32[]{:S(2)}) async-start(bf16[8,8,8,1536]{3,2,1,0:T(8,128)(2,1)} %bitcast.1), calls=%async_computation | async-start | bytes 3145728 | tf_op jit(solution)/shard_map/all_to_all | solution.py:139
  64.2 136.3 %reduce-scatter.2.cloned.1.call-start = ((), (), s32[]{:S(2)}) async-start(), calls=%async_computation.7 | async-start | bytes 10027008 | tf_op jit(solution)/shard_map/reduce_scatter | solution.py:206
  66.1 1.5 copy-start.9
  114.3 5.1 %copy-start.1 = (bf16[8,8,8,2304]{3,2,1,0:T(8,128)(2,1)}, bf16[8,8,8,2304]{3,2,1,0:T(8,128)(2,1)S(1)}, u32[]{:S(2)}) copy-start(bf16[8,8,8,2304]{3,2,1,0:T(8,128)(2,1)S(1)} %shard_map.104) | copy-start | bytes 7077892
  114.3 5.1 %copy-start.4 = (bf16[8,8,8,1536]{3,2,1,0:T(8,128)(2,1)S(1)}, bf16[8,8,8,1536]{3,2,1,0:T(8,128)(2,1)}, u32[]{:S(2)}) copy-start(bf16[8,8,8,1536]{3,2,1,0:T(8,128)(2,1)} %copy-done.3) | copy-start | bytes 4718596
  119.4 4.4 %copy-start.6 = (bf16[1536,768]{1,0:T(8,128)(2,1)S(1)}, bf16[1536,768]{1,0:T(8,128)(2,1)}, u32[]{:S(2)}) copy-start(bf16[1536,768]{1,0:T(8,128)(2,1)} %fusion.7) | copy-start | bytes 7077892
  128.4 84.0 %copy-start.2 = (bf16[8,8,8,2304]{3,2,1,0:T(8,128)(2,1)S(1)}, bf16[8,8,8,2304]{3,2,1,0:T(8,128)(2,1)}, u32[]{:S(2)}) copy-start(bf16[8,8,8,2304]{3,2,1,0:T(8,128)(2,1)} %copy-done.1) | copy-start | bytes 7077892
  128.5 84.0 %copy-start.10 = (f32[512]{0:T(512)S(1)}, f32[512]{0:T(512)}, u32[]{:S(2)}) copy-start(f32[512]{0:T(512)} %copy-done.9) | copy-start | bytes 6148
  202.5 27.1 %all-to-all-start.3 = ((bf16[16,48,384]{2,1,0:T(8,128)(2,1)}), bf16[16,48,384]{2,1,0:T(8,128)(2,1)S(1)}, u32[]{:S(2)}, u32[]{:S(2)}) async-start(bf16[16,48,384]{2,1,0:T(8,128)(2,1)} %bitcast.20), calls=%async_computation.4 | async-start | bytes 1179648 | tf_op jit(solution)/shard_map/all_to_all | solution.py:165
  212.5 7.5 %copy-start.5 = (bf16[8,8,8,1536]{3,2,1,0:T(8,128)(2,1)S(1)}, bf16[8,8,8,1536]{3,2,1,0:T(8,128)(2,1)}, u32[]{:S(2)}) copy-start(bf16[8,8,8,1536]{3,2,1,0:T(8,128)(2,1)} %copy-done.3) | copy-start | bytes 4718596
  229.6 45.4 %all-to-all-start.2 = ((bf16[8,8,8,1536]{3,2,1,0:T(8,128)(2,1)}), bf16[8,8,8,1536]{3,2,1,0:T(8,128)(2,1)S(1)}, u32[]{:S(2)}, u32[]{:S(2)}) async-start(bf16[8,8,8,1536]{3,2,1,0:T(8,128)(2,1)} %bitcast.12), calls=%async_computation.2 | async-start | bytes 3145728 | tf_op jit(solution)/shard_map/all_to_all | solution.py:146
  275.9 22.0 %all-to-all-start.4 = ((bf16[16,48,384]{2,1,0:T(8,128)(2,1)}), bf16[16,48,384]{2,1,0:T(8,128)(2,1)S(1)}, u32[]{:S(2)}, u32[]{:S(2)}) async-start(bf16[16,48,384]{2,1,0:T(8,128)(2,1)} %broadcast_in_dim.5), calls=%async_computation.5 | async-start | bytes 1179648 | tf_op jit(solution)/shard_map/all_to_all | solution.py:168
Sparse Core Ops, SparseCore 0:
  10.4 62.0 all-gather.1
  128.6 71.8 reduce-scatter.1
